TPU v7x, 256 devices: a whole 4x4x8 slice. The times are simulated.
256 devices in a mesh: grp: 8 (over x, core), row: 32 (over y, z).
Axes of the slice: x: 4, y: 4, z: 8, core: 2. Of those that a mesh axis runs over, the one named last changes fastest.
Arguments:
- features: bfloat16 [8192, 8192], P('row', 'grp'), may hold values from -0.0625 to 0.0625
- residual: float32 [8192, 576], P('row'), may hold values from -6 to 6
- precond: float32 [8192, 1024], P('grp'), as said below
Outputs:
- coefs: float32 [8192, 576], P('grp')
- section_resid: float32 [8, 8192, 576], P('grp', 'row')
Inputs may be any that keep to these rules, and one draw needn't show every extreme that they name: Each 1024 x 1024 block of precond is symmetric and positive definite.
All inputs are finite; a program needn't handle non-finite values.
Results may differ from a plain program's by a relative error of at most 0.009.
Values may be sent and summed in bfloat16 or wider, within the bound.
A program may use at most 64 MiB of HBM per device.

v0:
```python
import jax
import jax.numpy as jnp
from jax import lax
from jax.sharding import PartitionSpec as P


def from_behind(block, axis, distance):
    devices = range(lax.axis_size(axis))
    route = [(i - distance, i) for i in devices if i - distance in devices]
    return lax.ppermute(block, axis, route)


def chain_sweep(features, residual, precond):
    section_index = lax.axis_index("grp")
    section_count = lax.axis_size("grp")
    row_count, target_width = residual.shape
    block_width = features.shape[1]
    panel_count = 3
    panel_width = target_width // panel_count
    step_count = section_count + panel_count - 1

    def correlate(rounded):
        correlation = lax.dot_general(
            features, rounded, (((0,), (0,)), ((), ())), preferred_element_type=jnp.float32
        )
        correlation = lax.psum(correlation, "row")
        share = block_width // lax.axis_size("row")
        first = lax.axis_index("row") * share
        own_map = lax.dynamic_slice_in_dim(precond, first, share, 0)
        own_rows = jnp.dot(own_map, correlation, precision=lax.Precision.HIGHEST)
        return lax.all_gather(own_rows, "row", axis=0, tiled=True)

    def turn(turn_index, loop_state):
        current, coef_table, resid_table = loop_state
        position = turn_index - section_index
        inside = jnp.logical_and(position >= 0, position < panel_count)
        panel_slot = jnp.clip(position, 0, panel_count - 1) * panel_width
        fresh_panel = lax.dynamic_slice_in_dim(residual, panel_slot, panel_width, 1)
        current = jnp.where(section_index == 0, fresh_panel, current)
        rounded = current.astype(jnp.bfloat16)
        coefficient = correlate(rounded)
        updated = current - jnp.dot(
            features, coefficient.astype(jnp.bfloat16), preferred_element_type=jnp.float32
        )
        old_coef = lax.dynamic_slice_in_dim(coef_table, panel_slot, panel_width, 1)
        coef_table = lax.dynamic_update_slice_in_dim(
            coef_table, jnp.where(inside, coefficient, old_coef), panel_slot, 1
        )
        old_resid = lax.dynamic_slice_in_dim(resid_table, panel_slot, panel_width, 2)
        resid_table = lax.dynamic_update_slice_in_dim(
            resid_table, jnp.where(inside, updated[None], old_resid), panel_slot, 2
        )
        passed = from_behind(updated, "grp", 1)
        return (passed, coef_table, resid_table)

    start_state = (
        jnp.zeros((row_count, panel_width), jnp.float32),
        jnp.zeros((block_width, target_width), jnp.float32),
        jnp.zeros((1, row_count, target_width), jnp.float32),
    )
    final_state = lax.fori_loop(0, step_count, turn, start_state)
    return (final_state[1], final_state[2])


def local(features, residual, precond):
    return chain_sweep(features, residual, precond)


def solution(mesh):
    placed = (P("row", "grp"), P("row", None), P("grp", None))
    return jax.shard_map(
        local,
        mesh=mesh,
        in_specs=placed,
        out_specs=(P("grp", None), P("grp", "row", None)),
        check_vma=False,
    )
```

profile of v0, /device:TPU:7, one launch (start us, length us, event | category | flops | bytes accessed | tf_op | source)
XLA Modules:
  0.0 2117.2 jit_solution(15154932183782905294)
XLA Ops:
  9.8 2100.6 %while.18 = (s32[]{:T(128)}, f32[256,192]{0,1:T(8,128)S(1)}, f32[1024,576]{0,1:T(8,128)}, f32[1,256,576]{1,2,0:T(8,128)}, pred[]{:T(512)}, /*index=5*/s32[]{:T(1...) while((s32[]{:T(128)}, f32[256,192]{0,1:T(8,128)S(1)}, ...), condition=%wide.region_2.3_spmd, body=%wide.region_0.2_spmd.sunk | while | flops 277610496 | bytes 19809716 | solution.py:61
  9.8 2.1 convolution_bitcast_fusion.3
  13.4 147.4 %all-reduce.2.cloned.1.call-done = f32[1024,192]{0,1:T(8,128)} async-done(((f32[1024,192]{0,1:T(8,128)}), f32[1024,192]{0,1:T(8,128)}) %all-reduce.2.cloned.1.call-update) | async-done | bytes 786448 | tf_op jit(solution)/shard_map/while/body/eval_jaxpr/psum | solution.py:26
  162.8 36.9 %all_gather.9 = f32[1024,192]{1,0:T(8,128)S(1)} all-gather(f32[32,192]{1,0:T(8,128)S(1)} %fusion.23), channel_id=1, replica_groups=mesh['grp'=8,'row'=32] {'row'}, dimensions={0}, use_global_device_ids=true | all-gather | bytes 811008 | tf_op jit(solution)/shard_map/while/body/eval_jaxpr/all_gather | solution.py:31
  204.5 17.2 collective-permute-done
  225.3 145.5 %all-reduce.2.cloned.1.call-done = f32[1024,192]{0,1:T(8,128)} async-done(((f32[1024,192]{0,1:T(8,128)}), f32[1024,192]{0,1:T(8,128)}) %all-reduce.2.cloned.1.call-update) | async-done | bytes 786448 | tf_op jit(solution)/shard_map/while/body/eval_jaxpr/psum | solution.py:26
  372.8 36.9 %all_gather.9 = f32[1024,192]{1,0:T(8,128)S(1)} all-gather(f32[32,192]{1,0:T(8,128)S(1)} %fusion.23), channel_id=1, replica_groups=mesh['grp'=8,'row'=32] {'row'}, dimensions={0}, use_global_device_ids=true | all-gather | bytes 811008 | tf_op jit(solution)/shard_map/while/body/eval_jaxpr/all_gather | solution.py:31
  414.5 17.2 collective-permute-done
  435.3 145.5 %all-reduce.2.cloned.1.call-done = f32[1024,192]{0,1:T(8,128)} async-done(((f32[1024,192]{0,1:T(8,128)}), f32[1024,192]{0,1:T(8,128)}) %all-reduce.2.cloned.1.call-update) | async-done | bytes 786448 | tf_op jit(solution)/shard_map/while/body/eval_jaxpr/psum | solution.py:26
  582.8 36.9 %all_gather.9 = f32[1024,192]{1,0:T(8,128)S(1)} all-gather(f32[32,192]{1,0:T(8,128)S(1)} %fusion.23), channel_id=1, replica_groups=mesh['grp'=8,'row'=32] {'row'}, dimensions={0}, use_global_device_ids=true | all-gather | bytes 811008 | tf_op jit(solution)/shard_map/while/body/eval_jaxpr/all_gather | solution.py:31
  624.5 17.2 collective-permute-done
  645.3 145.2 %all-reduce.2.cloned.1.call-done = f32[1024,192]{0,1:T(8,128)} async-done(((f32[1024,192]{0,1:T(8,128)}), f32[1024,192]{0,1:T(8,128)}) %all-reduce.2.cloned.1.call-update) | async-done | bytes 786448 | tf_op jit(solution)/shard_map/while/body/eval_jaxpr/psum | solution.py:26
  792.5 36.9 %all_gather.9 = f32[1024,192]{1,0:T(8,128)S(1)} all-gather(f32[32,192]{1,0:T(8,128)S(1)} %fusion.23), channel_id=1, replica_groups=mesh['grp'=8,'row'=32] {'row'}, dimensions={0}, use_global_device_ids=true | all-gather | bytes 811008 | tf_op jit(solution)/shard_map/while/body/eval_jaxpr/all_gather | solution.py:31
  834.2 17.2 collective-permute-done
  855.0 145.2 %all-reduce.2.cloned.1.call-done = f32[1024,192]{0,1:T(8,128)} async-done(((f32[1024,192]{0,1:T(8,128)}), f32[1024,192]{0,1:T(8,128)}) %all-reduce.2.cloned.1.call-update) | async-done | bytes 786448 | tf_op jit(solution)/shard_map/while/body/eval_jaxpr/psum | solution.py:26
  1002.2 36.9 %all_gather.9 = f32[1024,192]{1,0:T(8,128)S(1)} all-gather(f32[32,192]{1,0:T(8,128)S(1)} %fusion.23), channel_id=1, replica_groups=mesh['grp'=8,'row'=32] {'row'}, dimensions={0}, use_global_device_ids=true | all-gather | bytes 811008 | tf_op jit(solution)/shard_map/while/body/eval_jaxpr/all_gather | solution.py:31
  1043.9 17.2 collective-permute-done
  1064.7 145.2 %all-reduce.2.cloned.1.call-done = f32[1024,192]{0,1:T(8,128)} async-done(((f32[1024,192]{0,1:T(8,128)}), f32[1024,192]{0,1:T(8,128)}) %all-reduce.2.cloned.1.call-update) | async-done | bytes 786448 | tf_op jit(solution)/shard_map/while/body/eval_jaxpr/psum | solution.py:26
  1211.9 36.9 %all_gather.9 = f32[1024,192]{1,0:T(8,128)S(1)} all-gather(f32[32,192]{1,0:T(8,128)S(1)} %fusion.23), channel_id=1, replica_groups=mesh['grp'=8,'row'=32] {'row'}, dimensions={0}, use_global_device_ids=true | all-gather | bytes 811008 | tf_op jit(solution)/shard_map/while/body/eval_jaxpr/all_gather | solution.py:31
  1253.6 17.2 collective-permute-done
  1274.4 145.5 %all-reduce.2.cloned.1.call-done = f32[1024,192]{0,1:T(8,128)} async-done(((f32[1024,192]{0,1:T(8,128)}), f32[1024,192]{0,1:T(8,128)}) %all-reduce.2.cloned.1.call-update) | async-done | bytes 786448 | tf_op jit(solution)/shard_map/while/body/eval_jaxpr/psum | solution.py:26
  1421.9 36.9 %all_gather.9 = f32[1024,192]{1,0:T(8,128)S(1)} all-gather(f32[32,192]{1,0:T(8,128)S(1)} %fusion.23), channel_id=1, replica_groups=mesh['grp'=8,'row'=32] {'row'}, dimensions={0}, use_global_device_ids=true | all-gather | bytes 811008 | tf_op jit(solution)/shard_map/while/body/eval_jaxpr/all_gather | solution.py:31
  1463.6 17.2 collective-permute-done
  1484.4 145.5 %all-reduce.2.cloned.1.call-done = f32[1024,192]{0,1:T(8,128)} async-done(((f32[1024,192]{0,1:T(8,128)}), f32[1024,192]{0,1:T(8,128)}) %all-reduce.2.cloned.1.call-update) | async-done | bytes 786448 | tf_op jit(solution)/shard_map/while/body/eval_jaxpr/psum | solution.py:26
  1631.9 36.9 %all_gather.9 = f32[1024,192]{1,0:T(8,128)S(1)} all-gather(f32[32,192]{1,0:T(8,128)S(1)} %fusion.23), channel_id=1, replica_groups=mesh['grp'=8,'row'=32] {'row'}, dimensions={0}, use_global_device_ids=true | all-gather | bytes 811008 | tf_op jit(solution)/shard_map/while/body/eval_jaxpr/all_gather | solution.py:31
  1673.5 17.2 collective-permute-done
  1694.4 145.5 %all-reduce.2.cloned.1.call-done = f32[1024,192]{0,1:T(8,128)} async-done(((f32[1024,192]{0,1:T(8,128)}), f32[1024,192]{0,1:T(8,128)}) %all-reduce.2.cloned.1.call-update) | async-done | bytes 786448 | tf_op jit(solution)/shard_map/while/body/eval_jaxpr/psum | solution.py:26
  1841.9 36.9 %all_gather.9 = f32[1024,192]{1,0:T(8,128)S(1)} all-gather(f32[32,192]{1,0:T(8,128)S(1)} %fusion.23), channel_id=1, replica_groups=mesh['grp'=8,'row'=32] {'row'}, dimensions={0}, use_global_device_ids=true | all-gather | bytes 811008 | tf_op jit(solution)/shard_map/while/body/eval_jaxpr/all_gather | solution.py:31
  1883.5 17.2 collective-permute-done
  1904.4 145.2 %all-reduce.2.cloned.1.call-done = f32[1024,192]{0,1:T(8,128)} async-done(((f32[1024,192]{0,1:T(8,128)}), f32[1024,192]{0,1:T(8,128)}) %all-reduce.2.cloned.1.call-update) | async-done | bytes 786448 | tf_op jit(solution)/shard_map/while/body/eval_jaxpr/psum | solution.py:26
  2051.6 36.9 %all_gather.9 = f32[1024,192]{1,0:T(8,128)S(1)} all-gather(f32[32,192]{1,0:T(8,128)S(1)} %fusion.23), channel_id=1, replica_groups=mesh['grp'=8,'row'=32] {'row'}, dimensions={0}, use_global_device_ids=true | all-gather | bytes 811008 | tf_op jit(solution)/shard_map/while/body/eval_jaxpr/all_gather | solution.py:31
  2093.2 17.2 collective-permute-done
  (114 shorter events, 104.2 us)
Async XLA Ops:
  7.2 2.6 copy-start
  9.8 151.0 %all-reduce.2.cloned.1.call-start = ((), (), s32[]{:S(2)}) async-start(), calls=%async_computation | async-start | bytes 1572864 | tf_op jit(solution)/shard_map/while/body/eval_jaxpr/psum | solution.py:26
  201.8 19.8 collective-permute-start
  221.6 149.2 %all-reduce.2.cloned.1.call-start = ((), (), s32[]{:S(2)}) async-start(), calls=%async_computation | async-start | bytes 1572864 | tf_op jit(solution)/shard_map/while/body/eval_jaxpr/psum | solution.py:26
  411.8 19.8 collective-permute-start
  431.6 149.2 %all-reduce.2.cloned.1.call-start = ((), (), s32[]{:S(2)}) async-start(), calls=%async_computation | async-start | bytes 1572864 | tf_op jit(solution)/shard_map/while/body/eval_jaxpr/psum | solution.py:26
  621.8 19.8 collective-permute-start
  641.6 148.9 %all-reduce.2.cloned.1.call-start = ((), (), s32[]{:S(2)}) async-start(), calls=%async_computation | async-start | bytes 1572864 | tf_op jit(solution)/shard_map/while/body/eval_jaxpr/psum | solution.py:26
  831.5 19.9 collective-permute-start
  851.3 148.9 %all-reduce.2.cloned.1.call-start = ((), (), s32[]{:S(2)}) async-start(), calls=%async_computation | async-start | bytes 1572864 | tf_op jit(solution)/shard_map/while/body/eval_jaxpr/psum | solution.py:26
  1041.2 19.8 collective-permute-start
  1061.0 148.9 %all-reduce.2.cloned.1.call-start = ((), (), s32[]{:S(2)}) async-start(), calls=%async_computation | async-start | bytes 1572864 | tf_op jit(solution)/shard_map/while/body/eval_jaxpr/psum | solution.py:26
  1250.9 19.9 collective-permute-start
  1270.7 149.2 %all-reduce.2.cloned.1.call-start = ((), (), s32[]{:S(2)}) async-start(), calls=%async_computation | async-start | bytes 1572864 | tf_op jit(solution)/shard_map/while/body/eval_jaxpr/psum | solution.py:26
  1460.9 19.8 collective-permute-start
  1480.7 149.2 %all-reduce.2.cloned.1.call-start = ((), (), s32[]{:S(2)}) async-start(), calls=%async_computation | async-start | bytes 1572864 | tf_op jit(solution)/shard_map/while/body/eval_jaxpr/psum | solution.py:26
  1670.8 19.8 collective-permute-start
  1690.7 149.2 %all-reduce.2.cloned.1.call-start = ((), (), s32[]{:S(2)}) async-start(), calls=%async_computation | async-start | bytes 1572864 | tf_op jit(solution)/shard_map/while/body/eval_jaxpr/psum | solution.py:26
  1880.9 19.8 collective-permute-start
  1900.7 148.8 %all-reduce.2.cloned.1.call-start = ((), (), s32[]{:S(2)}) async-start(), calls=%async_computation | async-start | bytes 1572864 | tf_op jit(solution)/shard_map/while/body/eval_jaxpr/psum | solution.py:26
  2090.5 19.9 collective-permute-start
Sparse Core Ops, SparseCore 0:
  13.9 146.8 all-reduce.1
  225.8 144.9 all-reduce.1
  435.8 144.9 all-reduce.1
  645.5 144.9 all-reduce.1
  855.2 144.9 all-reduce.1
  1064.9 144.9 all-reduce.1
  1274.9 144.9 all-reduce.1
  1484.9 144.9 all-reduce.1
  1694.9 144.9 all-reduce.1
  1904.6 144.9 all-reduce.1
where the time goes:
time: 2120 us
  waiting for transfers between devices  1630 us (77%)
  blocking collectives  369 us (17%)
  matrix products  61.7 us (3%)
  local copies, waits for them, and re-layouts  30.3 us (1%)
    psum x10, waiting for transfers between devices, correlate(): correlation = lax.psum(correlation, 'row')  1460 us
    all_gather x10, blocking collectives, correlate(): return lax.all_gather(own_rows, 'row', axis=0, tiled=True)  369 us
    ppermute x10, waiting for transfers between devices, from_behind(): return lax.ppermute(block, axis, route)  172 us
  transfers between devices with their start and end apart: 20, of which 20 were waited for; matrix products, arithmetic and copies ran while one was open for 1% of the time, Pallas kernels for 0%

commit v1 on v0

v1 whole, which is shorter than its diff:
```python
import jax
import jax.numpy as jnp
from jax import lax
from jax.experimental import pallas as pl
from jax.experimental.pallas import tpu as pltpu
from jax.sharding import PartitionSpec as P

MESH = pl.DeviceIdType.MESH
F32 = jnp.float32
BF16 = jnp.bfloat16

BLOCKS = 8
NY, NZ = 4, 8
ROWS = 256
BLK = 1024
TGT = 576
PANEL = TGT // BLOCKS
TILES = 5
WIDE = TILES * 16
LANES = BLK // NZ


def far_first():
    moves = [(dy, dz) for dy in range(NY) for dz in range(NZ) if (dy, dz) != (0, 0)]
    hops = lambda m: min(m[0], NY - m[0]) + min(m[1], NZ - m[1])
    return sorted(moves, key=hops, reverse=True)


def join(tiles):
    return jnp.concatenate(
        [tiles[z].reshape(WIDE, LANES) for z in range(NZ)], axis=1
    )


def sweep_kernel(
    feat_hbm, resid_hbm, prec_hbm, coef_out, sect_out,
    a_all, p_all, prec, resid, resid_t, chain, first, part, take, take_x,
    coef_all, coef_in, chain_in, coef_t, sect_t,
    load_sem, first_send, first_recv, own_send, fwd_send, p_recv, a_recv,
    rs_send, rs_send_x, rs_recv, rs_recv_x, ag_send, ag_send_x, ag_recv, ag_recv_x,
    c_send, c_recv, r_send, r_recv,
):
    g = lax.axis_index("grp")
    r = lax.axis_index("row")
    x, core = g // 2, lax.rem(g, 2)
    y, z = r // NZ, lax.rem(r, NZ)
    twice = y == lax.rem(z, NY)
    my_tile = lax.rem(y - z + 2 * NZ, NY)
    sibling = (2 * x + 1 - core, r)

    def remote(src, dst, send, recv, device):
        return pltpu.make_async_remote_copy(
            src_ref=src, dst_ref=dst, send_sem=send, recv_sem=recv,
            device_id=device, device_id_type=MESH,
        )

    def wait(ref, sem):
        pltpu.make_async_copy(ref, ref, sem).wait()

    loads = [
        pltpu.make_async_copy(resid_hbm, resid, load_sem.at[0]),
        pltpu.make_async_copy(feat_hbm, a_all.at[g], load_sem.at[1]),
        pltpu.make_async_copy(prec_hbm, prec, load_sem.at[2]),
    ]
    for copy in loads:
        copy.start()

    loads[0].wait()
    for j in range(5):
        low, high = 128 * j, min(128 * j + 128, TGT)
        resid_t[low:high, :] = resid[:, low:high].T
    resid_t[TGT:, :] = jnp.zeros((resid_t.shape[0] - TGT, ROWS), F32)
    chain[0] = resid_t[pl.ds(pl.multiple_of(g * PANEL, 8), WIDE), :]

    loads[1].wait()
    loads[2].wait()
    mine = a_all[g]

    def map_rows(j, carry):
        at = pl.ds(pl.multiple_of(j * 256, 256), 256)
        rows = prec[at, :]
        high = rows.astype(BF16)
        low = (rows - high.astype(F32)).astype(BF16)
        dims = (((1,), (1,)), ((), ()))
        out = lax.dot_general(mine, high, dims, preferred_element_type=F32)
        out += lax.dot_general(mine, low, dims, preferred_element_type=F32)
        p_all[g, :, at] = out.astype(BF16)
        return carry

    lax.fori_loop(0, BLK // 256, map_rows, 0)

    def store_part(ref, total):
        for k in range(NZ):
            ref[k] = total[:, k * LANES:(k + 1) * LANES].astype(BF16).reshape(
                TILES, 16, LANES
            )

    @pl.when(g == 0)
    def _():
        for to in (4, 5, 2, 3, 6, 7, 1, 0):
            panel = resid_t[PANEL * to:PANEL * to + WIDE, :].astype(BF16)
            total = jnp.dot(panel, p_all[0], preferred_element_type=F32)
            if to == 0:
                store_part(part.at[0], total)
            else:
                store_part(first.at[to - 1], total)
                remote(
                    first.at[to - 1], part.at[0], first_send, first_recv, (to, r)
                ).start()

    @pl.when(g != 0)
    def _():
        wait(part.at[0], first_recv)

    def own_targets():
        return [
            (lax.rem(g + 4, BLOCKS), r),
            (lax.rem(g + 2, BLOCKS), r),
            (lax.rem(g + 6, BLOCKS), r),
            sibling,
        ]

    def take_block(store, recv, sent, b):
        @pl.when(jnp.logical_and(lax.rem(b, 2) == core, b != g))
        def _():
            wait(store.at[b], recv.at[b])
            remote(store.at[b], store.at[b], sent, recv.at[b], sibling).start()

    def need_block(store, recv, b):
        @pl.when(lax.rem(b, 2) != core)
        def _():
            wait(store.at[b], recv.at[b])

    def wait_eight(sem, b):
        @pl.when(twice)
        def _():
            wait(take.at[b, pl.ds(0, 7)], sem)

        @pl.when(jnp.logical_not(twice))
        def _():
            wait(take.at[b, pl.ds(0, 8)], sem)

    moves = far_first()

    def block_step(b, carry):
        @pl.when(b > 0)
        def _():
            need_block(p_all, p_recv, b)
            total = jnp.dot(
                chain[b].astype(BF16), p_all[b], preferred_element_type=F32
            )
            store_part(part.at[b], total)

        def send_part_x(dz):
            zz = lax.rem(z + dz, NZ)
            yy = lax.rem(zz, NY)
            slot = lax.rem(yy - y + NY, NY) * NZ + dz
            remote(
                part.at[b, zz, 4], take_x.at[b, slot], rs_send_x.at[b],
                rs_recv_x.at[b], (g, yy * NZ + zz),
            ).start()

        for dz in (4, 3, 5, 2, 6, 1, 7):
            send_part_x(dz)

        @pl.when(jnp.logical_not(twice))
        def _():
            send_part_x(0)

        for dy, dz in moves:
            yy, zz = lax.rem(y + dy, NY), lax.rem(z + dz, NZ)
            tile = lax.rem(yy - zz + 2 * NZ, NY)
            remote(
                part.at[b, zz, tile], take.at[b, dy * NZ + dz], rs_send.at[b],
                rs_recv.at[b], (g, yy * NZ + zz),
            ).start()

        @pl.when(b == 0)
        def _():
            @pl.when(g > 0)
            def _():
                for to in own_targets():
                    remote(p_all.at[g], p_all.at[g], own_send.at[0], p_recv.at[g], to).start()

            for to in own_targets():
                remote(a_all.at[g], a_all.at[g], own_send.at[1], a_recv.at[g], to).start()

        take_block(a_all, a_recv, fwd_send.at[1], b)

        wait(take.at[b, pl.ds(1, 31)], rs_recv.at[b])
        total = part[b, z, my_tile].astype(F32)
        total += jnp.sum(take[b, 1:].astype(F32), axis=0)
        coef_all[b, z, my_tile] = total.astype(BF16)

        for dy, dz in moves:
            yy, zz = lax.rem(y + dy, NY), lax.rem(z + dz, NZ)
            remote(
                coef_all.at[b, z, my_tile], coef_all.at[b, z, my_tile],
                ag_send.at[b], ag_recv.at[b], (g, yy * NZ + zz),
            ).start()

        @pl.when(twice)
        def _():
            wait(take_x.at[b, pl.ds(1, 31)], rs_recv_x.at[b])
            more = part[b, z, 4].astype(F32)
            more += jnp.sum(take_x[b, 1:].astype(F32), axis=0)
            coef_all[b, z, 4] = more.astype(BF16)
            for dy, dz in moves:
                yy, zz = lax.rem(y + dy, NY), lax.rem(z + dz, NZ)
                remote(
                    coef_all.at[b, z, 4], coef_all.at[b, z, 4],
                    ag_send_x.at[b], ag_recv_x.at[b], (g, yy * NZ + zz),
                ).start()

        @pl.when(b < BLOCKS - 1)
        def _():
            take_block(p_all, p_recv, fwd_send.at[0], b + 1)

        need_block(a_all, a_recv, b)

        wait(take.at[b, pl.ds(1, 31)], ag_recv.at[b])
        wait_eight(ag_recv_x.at[b], b)

        @pl.when(b != g)
        def _():
            remote(coef_all.at[b], coef_in.at[g], c_send.at[b], c_recv.at[g], (b, r)).start()

        weights = join(coef_all[b])
        change = lax.dot_general(
            weights, a_all[b], (((1,), (1,)), ((), ())), preferred_element_type=F32
        )
        chain[b + 1] = chain[b] - change

        @pl.when(b != g)
        def _():
            remote(chain.at[b + 1], chain_in.at[g], r_send.at[b], r_recv.at[g], (b, r)).start()

        return carry

    lax.fori_loop(0, BLOCKS, block_step, 0)

    coef_in[g] = coef_all[g]
    chain_in[g] = chain[g + 1]
    for of in range(BLOCKS):
        @pl.when(g != of)
        def _():
            wait(coef_in.at[of], c_recv.at[of])

        at = slice(PANEL * of, PANEL * (of + 1))
        coef_t[at, :] = join(coef_in[of])[:PANEL].astype(F32)

    for k in range(NZ):
        at = slice(k * LANES, (k + 1) * LANES)
        coef_out[at, :] = coef_t[:, at].T[:, :TGT]

    for of in range(BLOCKS):
        @pl.when(g != of)
        def _():
            wait(chain_in.at[of], r_recv.at[of])

        sect_t[PANEL * of:PANEL * (of + 1), :] = chain_in[of][:PANEL]

    for k in range(ROWS // LANES):
        at = slice(k * LANES, (k + 1) * LANES)
        sect_out[at, :] = sect_t[:, at].T[:, :TGT]

    @pl.when(g == 0)
    def _():
        wait(first, first_send)

    @pl.when(g > 0)
    def _():
        wait(p_all.at[pl.ds(0, 4)], own_send.at[0])

    wait(a_all.at[pl.ds(0, 4)], own_send.at[1])
    wait(a_all.at[pl.ds(0, 3)], fwd_send.at[1])

    @pl.when(jnp.logical_and(core == 0, x > 0))
    def _():
        wait(p_all.at[pl.ds(0, 2)], fwd_send.at[0])

    @pl.when(jnp.logical_or(core == 1, x == 0))
    def _():
        wait(p_all.at[pl.ds(0, 3)], fwd_send.at[0])

    def drain(b, carry):
        wait(take.at[b, pl.ds(1, 31)], rs_send.at[b])
        wait(take.at[b, pl.ds(1, 31)], ag_send.at[b])
        wait_eight(rs_send_x.at[b], b)

        @pl.when(twice)
        def _():
            wait(take.at[b, pl.ds(1, 31)], ag_send_x.at[b])

        @pl.when(b != g)
        def _():
            wait(coef_all.at[b], c_send.at[b])
            wait(chain.at[b + 1], r_send.at[b])

        return carry

    lax.fori_loop(0, BLOCKS, drain, 0)


def local(features, residual, precond):
    tiles = (NZ, TILES, 16, LANES)
    sem = pltpu.SemaphoreType.DMA
    hbm = pl.BlockSpec(memory_space=pl.ANY)
    vmem = pl.BlockSpec(memory_space=pltpu.VMEM)
    coefs, section = pl.pallas_call(
        sweep_kernel,
        name="block_sweep",
        out_shape=(
            jax.ShapeDtypeStruct((BLK, TGT), F32),
            jax.ShapeDtypeStruct((ROWS, TGT), F32),
        ),
        in_specs=[hbm] * 3,
        out_specs=(vmem, vmem),
        scratch_shapes=[
            pltpu.VMEM((BLOCKS, ROWS, BLK), BF16),
            pltpu.VMEM((BLOCKS, ROWS, BLK), BF16),
            pltpu.VMEM((BLK, BLK), F32),
            pltpu.VMEM((ROWS, TGT), F32),
            pltpu.VMEM((640, ROWS), F32),
            pltpu.VMEM((BLOCKS + 1, WIDE, ROWS), F32),
            pltpu.VMEM((BLOCKS - 1,) + tiles, BF16),
            pltpu.VMEM((BLOCKS,) + tiles, BF16),
            pltpu.VMEM((BLOCKS, 32, 16, LANES), BF16),
            pltpu.VMEM((BLOCKS, 32, 16, LANES), BF16),
            pltpu.VMEM((BLOCKS,) + tiles, BF16),
            pltpu.VMEM((BLOCKS,) + tiles, BF16),
            pltpu.VMEM((BLOCKS, WIDE, ROWS), F32),
            pltpu.VMEM((640, BLK), F32),
            pltpu.VMEM((640, ROWS), F32),
            sem((3,)), sem, sem, sem((2,)), sem((2,)), sem((BLOCKS,)), sem((BLOCKS,)),
        ] + [sem((BLOCKS,))] * 12,
        compiler_params=pltpu.CompilerParams(
            has_side_effects=True, vmem_limit_bytes=48 * 2**20
        ),
        cost_estimate=pl.CostEstimate(
            flops=2 * 10**9, bytes_accessed=8 * 10**6, transcendentals=0
        ),
    )(features, residual, precond)
    return coefs, section[None]


def solution(mesh):
    placed = (P("row", "grp"), P("row", None), P("grp", None))
    return jax.shard_map(
        local,
        mesh=mesh,
        in_specs=placed,
        out_specs=(P("grp", None), P("grp", "row", None)),
        check_vma=False,
    )
```

time: 2120 us -> 185 us (0.09)
  waiting for transfers between devices: 1630 us -> 0 us
  blocking collectives: 369 us -> 0 us
  Pallas kernels: 0 us -> 177 us
  matrix products: 61.7 us -> 0 us
  local copies, waits for them, and re-layouts: 30.3 us -> 7.29 us
    psum x10 -> x0, waiting for transfers between devices: 1460 us -> none  [correlate(): correlation = lax.psum(correlation, 'row')]
    all_gather x10 -> x0, blocking collectives: 369 us -> none  [correlate(): return lax.all_gather(own_rows, 'row', axis=0, tiled=True)]
    pallas_call x0 -> x1, Pallas kernels: none -> 177 us  [local(): pl.pallas_call(sweep_kernel, name='block_sweep', out_shape=(jax.ShapeDtyp...]
    ppermute x10 -> x0, waiting for transfers between devices: 172 us -> none  [from_behind(): return lax.ppermute(block, axis, route)]
    dot_general x30 -> x0, matrix products: 61.7 us -> none  [the longest x10 21 us: correlate(): lax.dot_general(features, rounded, (((0,), (0,)), ((), ())), preferred_el...]
  transfers between devices with their start and end apart: 20 -> 0, of which waited for: 20 -> 0; matrix products, arithmetic and copies ran while one was open for 1% -> 0% of each run, Pallas kernels for 0% -> 0%
where the time goes in v1:
time: 185 us
  Pallas kernels  177 us (96%)
  local copies, waits for them, and re-layouts  7.29 us (4%)
    pallas_call x1, Pallas kernels, local(): pl.pallas_call(sweep_kernel, name='block_sweep', out_shape=(jax.ShapeDtyp...  177 us
    unnamed x7, local copies, waits for them, and re-layouts  7.29 us

profile of v1, /device:TPU:7, one launch (start us, length us, event | category | flops | bytes accessed | tf_op | source)
XLA Modules:
  0.0 184.6 jit_solution(14794825616646299757)
XLA Ops:
  0.6 2.1 %copy.5.resid_hbm = f32[256,576]{1,0:T(8,128)} copy(f32[256,576]{0,1:T(8,128)} %param.4) | data formatting | bytes 1179648 | tf_op args[1]
  2.8 0.0 copy-start
  2.8 1.1 copy-done
  3.9 0.0 copy-start.1
  3.9 1.0 copy-done.1
  4.9 176.7 %block_sweep.1 = (f32[1024,576]{1,0:T(8,128)S(1)}, f32[256,576]{1,0:T(8,128)S(1)}) custom-call(bf16[256,1024]{1,0:T(8,128)(2,1)S(1)} %copy-done.1, f32[256,576]{1,0:T(8,128)S(1)} %copy-done, f32[1024,1024]{1,0:T(8,128)} %prec_hbm.1), custom_call_target="tpu_custom_call" | custom-call | flops 2000000000 | bytes 8000000 | tf_op jit(solution)/shard_map/block_sweep/pallas_call | solution.py:310
  181.6 2.0 %copy.6 = f32[1024,576]{0,1:T(8,128)} copy(f32[1024,576]{1,0:T(8,128)S(1)} %get-tuple-element.6) | data formatting | bytes 4718592
  183.6 1.0 copy.7
Async XLA Ops:
  2.8 1.1 copy-start
  3.9 1.0 copy-start.1

commit v2 on v1

v2 whole, which is shorter than its diff:
```python
import jax
import jax.numpy as jnp
from jax import lax
from jax.experimental import pallas as pl
from jax.experimental.pallas import tpu as pltpu
from jax.sharding import PartitionSpec as P

MESH = pl.DeviceIdType.MESH
F32 = jnp.float32
BF16 = jnp.bfloat16

BLOCKS = 8
NY, NZ = 4, 8
ROWS = 256
BLK = 1024
TGT = 576
PANEL = TGT // BLOCKS
TILES = 5
WIDE = TILES * 16
LANES = BLK // NZ
CHUNKS = 4


def far_first():
    moves = [(dy, dz) for dy in range(NY) for dz in range(NZ) if (dy, dz) != (0, 0)]
    hops = lambda m: min(m[0], NY - m[0]) + min(m[1], NZ - m[1])
    return sorted(moves, key=hops, reverse=True)


def join(tiles):
    return jnp.concatenate(
        [tiles[z].reshape(WIDE, LANES) for z in range(NZ)], axis=1
    )


def sweep_kernel(
    feat_hbm, resid_hbm, prec_hbm, coef_out, sect_out,
    a_all, p_all, prec, resid, chain, rounded, first, part, take,
    coef_all, coef_in, chain_in,
    load_sem, first_send, first_recv, own_send, fwd_send, p_recv, a_recv,
    rs_send, rs_recv, ag_send, ag_recv, c_send, c_recv, r_send, r_recv,
):
    g = lax.axis_index("grp")
    r = lax.axis_index("row")
    x, core = g // 2, lax.rem(g, 2)
    y, z = r // NZ, lax.rem(r, NZ)
    twice = y == lax.rem(z, NY)
    my_tile = lax.rem(y - z + 2 * NZ, NY) + 1
    sibling = (2 * x + 1 - core, r)

    def remote(src, dst, send, recv, device):
        return pltpu.make_async_remote_copy(
            src_ref=src, dst_ref=dst, send_sem=send, recv_sem=recv,
            device_id=device, device_id_type=MESH,
        )

    def wait(ref, sem):
        pltpu.make_async_copy(ref, ref, sem).wait()

    chunk = BLK // CHUNKS
    loads = [
        pltpu.make_async_copy(feat_hbm, a_all.at[g], load_sem.at[0]),
        pltpu.make_async_copy(resid_hbm, resid.at[pl.ds(0, TGT)], load_sem.at[1]),
    ] + [
        pltpu.make_async_copy(
            prec_hbm.at[pl.ds(j * chunk, chunk)], prec.at[pl.ds(j * chunk, chunk)],
            load_sem.at[2 + j],
        )
        for j in range(CHUNKS)
    ]
    for copy in loads:
        copy.start()

    barrier = pltpu.get_barrier_semaphore()
    moves = far_first()
    others = [(g, lax.rem(y + dy, NY) * NZ + lax.rem(z + dz, NZ)) for dy, dz in moves]
    others += [(lax.rem(g + d, BLOCKS), r) for d in range(1, BLOCKS)]
    for other in others:
        pl.semaphore_signal(barrier, inc=1, device_id=other, device_id_type=MESH)

    def panel(of):
        low = of * PANEL if isinstance(of, int) else pl.multiple_of(of * PANEL, 8)
        return jnp.concatenate(
            [resid[pl.ds(low + 64, 16), :], resid[pl.ds(low, 64), :]], axis=0
        )

    resid[TGT:, :] = jnp.zeros((resid.shape[0] - TGT, ROWS), F32)
    loads[0].wait()
    loads[1].wait()
    chain[...] = panel(g)
    mine = a_all[g]

    def store_part(ref, total):
        for k in range(total.shape[1] // LANES):
            ref[k] = total[:, k * LANES:(k + 1) * LANES].astype(BF16).reshape(
                TILES, 16, LANES
            )

    for j in range(CHUNKS):
        at = slice(j * chunk, (j + 1) * chunk)
        loads[2 + j].wait()
        rows = prec[at, :]
        high = rows.astype(BF16)
        low = (rows - high.astype(F32)).astype(BF16)
        dims = (((1,), (1,)), ((), ()))
        out = lax.dot_general(mine, high, dims, preferred_element_type=F32)
        out += lax.dot_general(mine, low, dims, preferred_element_type=F32)
        mapped = out.astype(BF16)
        p_all[g, :, at] = mapped
        if j == 0:
            pl.semaphore_wait(barrier, len(others))

        @pl.when(g == 0)
        def _():
            groups = pl.ds(j * chunk // LANES, chunk // LANES)
            for to in (4, 5, 2, 6, 3, 7, 1, 0):
                total = jnp.dot(
                    panel(to).astype(BF16), mapped, preferred_element_type=F32
                )
                if to == 0:
                    store_part(part.at[0, groups], total)
                else:
                    store_part(first.at[to - 1, groups], total)
                    remote(
                        first.at[to - 1, groups], part.at[0, groups],
                        first_send, first_recv, (to, r),
                    ).start()

    @pl.when(g != 0)
    def _():
        wait(part.at[0], first_recv)

    def own_targets():
        return [
            (lax.rem(g + 4, BLOCKS), r),
            (lax.rem(g + 2, BLOCKS), r),
            (lax.rem(g + 6, BLOCKS), r),
            sibling,
        ]

    def take_block(store, recv, sent, b):
        @pl.when(jnp.logical_and(lax.rem(b, 2) == core, b != g))
        def _():
            wait(store.at[b], recv.at[b])
            remote(store.at[b], store.at[b], sent, recv.at[b], sibling).start()

    def need_block(store, recv, b):
        @pl.when(lax.rem(b, 2) != core)
        def _():
            wait(store.at[b], recv.at[b])

    def send_own(store, recv, sent):
        for to in own_targets():
            remote(store.at[g], store.at[g], sent, recv.at[g], to).start()

    @pl.when(g == 0)
    def _():
        send_own(a_all, a_recv, own_send.at[1])

    def wait_each(sem):
        @pl.when(twice)
        def _():
            wait(take.at[0, pl.ds(1, 31)], sem)

        @pl.when(jnp.logical_not(twice))
        def _():
            wait(take.at[0, pl.ds(1, 31), 0], sem)

    def wait_rest(sem):
        @pl.when(twice)
        def _():
            wait(take.at[0, pl.ds(1, 19)], sem)

        @pl.when(jnp.logical_not(twice))
        def _():
            wait(take.at[pl.ds(0, 3), pl.ds(0, 13), 0], sem)

    def block_step(b, carry):
        @pl.when(b > 0)
        def _():
            need_block(p_all, p_recv, b)
            total = jnp.dot(rounded[b], p_all[b], preferred_element_type=F32)
            store_part(part.at[b], total)

        for dy, dz in moves:
            yy, zz = lax.rem(y + dy, NY), lax.rem(z + dz, NZ)
            tile = lax.rem(yy - zz + 2 * NZ, NY) + 1
            to, slot = (g, yy * NZ + zz), dy * NZ + dz

            @pl.when(tile == 1)
            def _():
                pair = pl.ds(0, 2)
                remote(
                    part.at[b, zz, pair], take.at[b, slot, pair], rs_send.at[b],
                    rs_recv.at[b], to,
                ).start()

            @pl.when(tile > 1)
            def _():
                remote(
                    part.at[b, zz, tile], take.at[b, slot, 1], rs_send.at[b],
                    rs_recv.at[b], to,
                ).start()

        @pl.when(jnp.logical_or(g == b + 2, jnp.logical_and(b == 0, g == 1)))
        def _():
            send_own(p_all, p_recv, own_send.at[0])
            send_own(a_all, a_recv, own_send.at[1])

        take_block(a_all, a_recv, fwd_send.at[1], b)

        wait_each(rs_recv.at[b])

        def add_up(tile, slot):
            total = part[b, z, tile].astype(F32)
            total += jnp.sum(take[b, 1:, slot].astype(F32), axis=0)
            coef_all[b, z, tile] = total.astype(BF16)

        def spread(ref):
            for dy, dz in moves:
                yy, zz = lax.rem(y + dy, NY), lax.rem(z + dz, NZ)
                remote(ref, ref, ag_send.at[b], ag_recv.at[b], (g, yy * NZ + zz)).start()

        add_up(my_tile, 1)

        @pl.when(twice)
        def _():
            add_up(0, 0)
            spread(coef_all.at[b, z, pl.ds(0, 2)])

        @pl.when(jnp.logical_not(twice))
        def _():
            spread(coef_all.at[b, z, my_tile])

        @pl.when(b < BLOCKS - 1)
        def _():
            take_block(p_all, p_recv, fwd_send.at[0], b + 1)

        need_block(a_all, a_recv, b)

        wait_rest(ag_recv.at[b])

        @pl.when(b != g)
        def _():
            remote(coef_all.at[b], coef_in.at[g], c_send.at[b], c_recv.at[g], (b, r)).start()

        weights = join(coef_all[b])
        change = lax.dot_general(
            weights, a_all[b], (((1,), (1,)), ((), ())), preferred_element_type=F32
        )
        left = chain[...] - change
        chain[...] = left
        rounded[b + 1] = left.astype(BF16)

        @pl.when(b != g)
        def _():
            remote(rounded.at[b + 1], chain_in.at[g], r_send.at[b], r_recv.at[g], (b, r)).start()

        return carry

    lax.fori_loop(0, BLOCKS, block_step, 0)

    coef_in[g] = coef_all[g]
    chain_in[g] = rounded[g + 1]

    def unpack(out, of, rows):
        rows = rows.astype(F32)
        out[PANEL * of:PANEL * of + 64, :] = rows[16:]
        out[PANEL * of + 64:PANEL * of + 72, :] = rows[:8]

    for of in range(BLOCKS):
        @pl.when(g != of)
        def _():
            wait(coef_in.at[of], c_recv.at[of])

        unpack(coef_out, of, join(coef_in[of]))

    for of in range(BLOCKS):
        @pl.when(g != of)
        def _():
            wait(chain_in.at[of], r_recv.at[of])

        unpack(sect_out, of, chain_in[of])

    @pl.when(g == 0)
    def _():
        wait(first, first_send)

    @pl.when(g > 0)
    def _():
        wait(p_all.at[pl.ds(0, 4)], own_send.at[0])

    wait(a_all.at[pl.ds(0, 4)], own_send.at[1])
    wait(a_all.at[pl.ds(0, 3)], fwd_send.at[1])

    @pl.when(jnp.logical_and(core == 0, x > 0))
    def _():
        wait(p_all.at[pl.ds(0, 2)], fwd_send.at[0])

    @pl.when(jnp.logical_or(core == 1, x == 0))
    def _():
        wait(p_all.at[pl.ds(0, 3)], fwd_send.at[0])

    def drain(b, carry):
        wait_rest(rs_send.at[b])
        wait_each(ag_send.at[b])

        @pl.when(b != g)
        def _():
            wait(coef_all.at[b], c_send.at[b])
            wait(rounded.at[b + 1], r_send.at[b])

        return carry

    lax.fori_loop(0, BLOCKS, drain, 0)


def local(features, residual, precond):
    tiles = (NZ, TILES, 16, LANES)
    sem = pltpu.SemaphoreType.DMA
    hbm = pl.BlockSpec(memory_space=pl.ANY)
    vmem = pl.BlockSpec(memory_space=pltpu.VMEM)
    coefs, section = pl.pallas_call(
        sweep_kernel,
        name="block_sweep",
        out_shape=(
            jax.ShapeDtypeStruct((TGT, BLK), F32),
            jax.ShapeDtypeStruct((TGT, ROWS), F32),
        ),
        in_specs=[hbm] * 3,
        out_specs=(vmem, vmem),
        scratch_shapes=[
            pltpu.VMEM((BLOCKS, ROWS, BLK), BF16),
            pltpu.VMEM((BLOCKS, ROWS, BLK), BF16),
            pltpu.VMEM((BLK, BLK), F32),
            pltpu.VMEM((592, ROWS), F32),
            pltpu.VMEM((WIDE, ROWS), F32),
            pltpu.VMEM((BLOCKS + 1, WIDE, ROWS), BF16),
            pltpu.VMEM((BLOCKS - 1,) + tiles, BF16),
            pltpu.VMEM((BLOCKS,) + tiles, BF16),
            pltpu.VMEM((BLOCKS, 32, 2, 16, LANES), BF16),
            pltpu.VMEM((BLOCKS,) + tiles, BF16),
            pltpu.VMEM((BLOCKS,) + tiles, BF16),
            pltpu.VMEM((BLOCKS, WIDE, ROWS), BF16),
            sem((2 + CHUNKS,)), sem, sem, sem((2,)), sem((2,)),
            sem((BLOCKS,)), sem((BLOCKS,)),
        ] + [sem((BLOCKS,))] * 8,
        compiler_params=pltpu.CompilerParams(
            collective_id=0, has_side_effects=True, vmem_limit_bytes=48 * 2**20
        ),
        cost_estimate=pl.CostEstimate(
            flops=2 * 10**9, bytes_accessed=8 * 10**6, transcendentals=0
        ),
    )(features, residual.T, precond)
    return coefs.T, section.T[None]


def solution(mesh):
    placed = (P("row", "grp"), P("row", None), P("grp", None))
    return jax.shard_map(
        local,
        mesh=mesh,
        in_specs=placed,
        out_specs=(P("grp", None), P("grp", "row", None)),
        check_vma=False,
    )
```

time: 185 us -> 165 us (0.89)
  Pallas kernels: 177 us -> 159 us
  local copies, waits for them, and re-layouts: 7.29 us -> 4.32 us
    pallas_call x1, Pallas kernels: 177 us -> 159 us  [local(): pl.pallas_call(sweep_kernel, name='block_sweep', out_shape=(jax.ShapeDtyp...]
    unnamed x7 -> x6, local copies, waits for them, and re-layouts: 7.29 us -> 4.32 us
where the time goes in v2:
time: 165 us; the launch traced here: 164 us
  Pallas kernels  159 us (96%)
  local copies, waits for them, and re-layouts  4.32 us (3%)
    pallas_call x1, Pallas kernels, local(): pl.pallas_call(sweep_kernel, name='block_sweep', out_shape=(jax.ShapeDtyp...  159 us
    unnamed x6, local copies, waits for them, and re-layouts  4.32 us

profile of v2, /device:TPU:7, one launch (start us, length us, event | category | flops | bytes accessed | tf_op | source)
XLA Modules:
  0.0 164.3 jit_solution(7133040136823562092)
XLA Ops:
  0.6 0.0 copy-start
  0.6 1.1 copy-done
  1.7 0.0 copy-start.1
  1.7 1.0 copy-done.1
  2.7 159.4 %block_sweep.1 = (f32[576,1024]{1,0:T(8,128)S(1)}, f32[576,256]{1,0:T(8,128)S(1)}) custom-call(bf16[256,1024]{1,0:T(8,128)(2,1)S(1)} %copy-done.1, f32[576,256]{1,0:T(8,128)S(1)} %bitcast.7, f32[1024,1024]{1,0:T(8,128)} %prec_hbm.1), custom_call_target="tpu_custom_call" | custom-call | flops 2000000000 | bytes 8000000 | tf_op jit(solution)/shard_map/block_sweep/pallas_call | solution.py:323
  162.1 1.4 copy.7
  163.5 0.8 copy.8
Async XLA Ops:
  0.6 1.1 copy-start
  1.7 1.0 copy-start.1

commit v3 on v2

--- a/solution.py
+++ b/solution.py
@@ -96,6 +96,40 @@
                 TILES, 16, LANES
             )
 
+    right, left = lax.rem(g + 2, BLOCKS), lax.rem(g + 6, BLOCKS)
+
+    def send_own(store, recv, sent):
+        for to in ((right, r), (left, r), sibling):
+            remote(store.at[g], store.at[g], sent, recv.at[g], to).start()
+
+    def same_core(b, distance):
+        return jnp.logical_and(
+            lax.rem(b, 2) == core, lax.rem(x - b // 2 + 4, 4) == distance
+        )
+
+    def pass_on(store, recv, sent, b):
+        for distance, onward in ((1, right), (3, left)):
+            @pl.when(same_core(b, distance))
+            def _():
+                wait(store.at[b], recv.at[b])
+                half = store.at[b, pl.ds(0 if distance == 1 else ROWS // 2, ROWS // 2)]
+                remote(half, half, sent, recv.at[b], (onward, r)).start()
+                remote(store.at[b], store.at[b], sent, recv.at[b], sibling).start()
+
+    def pass_across(store, recv, sent, b):
+        @pl.when(same_core(b, 2))
+        def _():
+            wait(store.at[b], recv.at[b])
+            remote(store.at[b], store.at[b], sent, recv.at[b], sibling).start()
+
+    def need_block(store, recv, b):
+        @pl.when(lax.rem(b, 2) != core)
+        def _():
+            wait(store.at[b], recv.at[b])
+
+    a_way = (a_all, a_recv, fwd_send.at[1])
+    p_way = (p_all, p_recv, fwd_send.at[0])
+
     for j in range(CHUNKS):
         at = slice(j * chunk, (j + 1) * chunk)
         loads[2 + j].wait()
@@ -110,6 +144,10 @@
         if j == 0:
             pl.semaphore_wait(barrier, len(others))
 
+            @pl.when(g > 1)
+            def _():
+                send_own(a_all, a_recv, own_send.at[1])
+
         @pl.when(g == 0)
         def _():
             groups = pl.ds(j * chunk // LANES, chunk // LANES)
@@ -126,34 +164,19 @@
                         first_send, first_recv, (to, r),
                     ).start()
 
+    @pl.when(g > 1)
+    def _():
+        send_own(p_all, p_recv, own_send.at[0])
+
     @pl.when(g != 0)
     def _():
         wait(part.at[0], first_recv)
 
-    def own_targets():
-        return [
-            (lax.rem(g + 4, BLOCKS), r),
-            (lax.rem(g + 2, BLOCKS), r),
-            (lax.rem(g + 6, BLOCKS), r),
-            sibling,
-        ]
-
-    def take_block(store, recv, sent, b):
-        @pl.when(jnp.logical_and(lax.rem(b, 2) == core, b != g))
-        def _():
-            wait(store.at[b], recv.at[b])
-            remote(store.at[b], store.at[b], sent, recv.at[b], sibling).start()
-
-    def need_block(store, recv, b):
-        @pl.when(lax.rem(b, 2) != core)
-        def _():
-            wait(store.at[b], recv.at[b])
-
-    def send_own(store, recv, sent):
-        for to in own_targets():
-            remote(store.at[g], store.at[g], sent, recv.at[g], to).start()
-
-    @pl.when(g == 0)
+    @pl.when(g == 1)
+    def _():
+        send_own(p_all, p_recv, own_send.at[0])
+
+    @pl.when(g < 2)
     def _():
         send_own(a_all, a_recv, own_send.at[1])
 
@@ -202,12 +225,17 @@
                     rs_recv.at[b], to,
                 ).start()
 
-        @pl.when(jnp.logical_or(g == b + 2, jnp.logical_and(b == 0, g == 1)))
-        def _():
-            send_own(p_all, p_recv, own_send.at[0])
-            send_own(a_all, a_recv, own_send.at[1])
-
-        take_block(a_all, a_recv, fwd_send.at[1], b)
+        @pl.when(b == 0)
+        def _():
+            pass_on(*a_way, b)
+
+        @pl.when(b > 0)
+        def _():
+            pass_across(*a_way, b)
+
+            @pl.when(b < BLOCKS - 1)
+            def _():
+                pass_on(*p_way, b + 1)
 
         wait_each(rs_recv.at[b])
 
@@ -232,9 +260,15 @@
         def _():
             spread(coef_all.at[b, z, my_tile])
 
+        @pl.when(b == 0)
+        def _():
+            pass_across(*a_way, b)
+            pass_on(*p_way, b + 1)
+
         @pl.when(b < BLOCKS - 1)
         def _():
-            take_block(p_all, p_recv, fwd_send.at[0], b + 1)
+            pass_across(*p_way, b + 1)
+            pass_on(*a_way, b + 1)
 
         need_block(a_all, a_recv, b)
 
@@ -248,9 +282,9 @@
         change = lax.dot_general(
             weights, a_all[b], (((1,), (1,)), ((), ())), preferred_element_type=F32
         )
-        left = chain[...] - change
-        chain[...] = left
-        rounded[b + 1] = left.astype(BF16)
+        remaining = chain[...] - change
+        chain[...] = remaining
+        rounded[b + 1] = remaining.astype(BF16)
 
         @pl.when(b != g)
         def _():
@@ -288,18 +322,22 @@
 
     @pl.when(g > 0)
     def _():
-        wait(p_all.at[pl.ds(0, 4)], own_send.at[0])
-
-    wait(a_all.at[pl.ds(0, 4)], own_send.at[1])
-    wait(a_all.at[pl.ds(0, 3)], fwd_send.at[1])
-
-    @pl.when(jnp.logical_and(core == 0, x > 0))
-    def _():
-        wait(p_all.at[pl.ds(0, 2)], fwd_send.at[0])
+        wait(p_all.at[pl.ds(0, 3)], own_send.at[0])
+
+    wait(a_all.at[pl.ds(0, 3)], own_send.at[1])
+    wait(a_all.at[pl.ds(0, 4)], fwd_send.at[1])
 
     @pl.when(jnp.logical_or(core == 1, x == 0))
     def _():
+        wait(p_all.at[pl.ds(0, 4)], fwd_send.at[0])
+
+    @pl.when(jnp.logical_and(core == 0, x == 2))
+    def _():
         wait(p_all.at[pl.ds(0, 3)], fwd_send.at[0])
+
+    @pl.when(jnp.logical_and(core == 0, lax.rem(x, 2) == 1))
+    def _():
+        wait(p_all.at[pl.ds(0, 5), pl.ds(0, ROWS // 2)], fwd_send.at[0])
 
     def drain(b, carry):
         wait_rest(rs_send.at[b])

time: 165 us -> 152 us (0.921)
  Pallas kernels: 159 us -> 147 us
    pallas_call x1, Pallas kernels: 159 us -> 147 us  [local(): pl.pallas_call(sweep_kernel, name='block_sweep', out_shape=(jax.ShapeDtyp...]
where the time goes in v3:
time: 152 us; the launch traced here: 151 us
  Pallas kernels  147 us (97%)
  local copies, waits for them, and re-layouts  4.32 us (3%)
    pallas_call x1, Pallas kernels, local(): pl.pallas_call(sweep_kernel, name='block_sweep', out_shape=(jax.ShapeDtyp...  147 us
    unnamed x6, local copies, waits for them, and re-layouts  4.32 us

profile of v3, /device:TPU:7, one launch (start us, length us, event | category | flops | bytes accessed | tf_op | source)
XLA Modules:
  0.0 151.5 jit_solution(5988018525763982872)
XLA Ops:
  0.6 0.0 copy-start
  0.6 1.1 copy-done
  1.7 0.0 copy-start.1
  1.7 1.0 copy-done.1
  2.7 146.5 %block_sweep.1 = (f32[576,1024]{1,0:T(8,128)S(1)}, f32[576,256]{1,0:T(8,128)S(1)}) custom-call(bf16[256,1024]{1,0:T(8,128)(2,1)S(1)} %copy-done.1, f32[576,256]{1,0:T(8,128)S(1)} %bitcast.7, f32[1024,1024]{1,0:T(8,128)} %prec_hbm.1), custom_call_target="tpu_custom_call" | custom-call | flops 2000000000 | bytes 8000000 | tf_op jit(solution)/shard_map/block_sweep/pallas_call | solution.py:361
  149.3 1.4 copy.7
  150.7 0.8 copy.8
Async XLA Ops:
  0.6 1.1 copy-start
  1.7 1.0 copy-start.1

commit v4 on v3

--- a/solution.py
+++ b/solution.py
@@ -19,6 +19,9 @@
 WIDE = TILES * 16
 LANES = BLK // NZ
 CHUNKS = 4
+
+CHAINS = ((0, 3), (3, 2))
+TURNS = ({0: 1, 1: 2, 2: 0}, {3: 3, 0: 4})
 
 
 def far_first():
@@ -44,8 +47,7 @@
     r = lax.axis_index("row")
     x, core = g // 2, lax.rem(g, 2)
     y, z = r // NZ, lax.rem(r, NZ)
-    twice = y == lax.rem(z, NY)
-    my_tile = lax.rem(y - z + 2 * NZ, NY) + 1
+    my_class = lax.rem(y - z + 2 * NZ, NY)
     sibling = (2 * x + 1 - core, r)
 
     def remote(src, dst, send, recv, device):
@@ -180,85 +182,105 @@
     def _():
         send_own(a_all, a_recv, own_send.at[1])
 
-    def wait_each(sem):
-        @pl.when(twice)
-        def _():
-            wait(take.at[0, pl.ds(1, 31)], sem)
-
-        @pl.when(jnp.logical_not(twice))
-        def _():
-            wait(take.at[0, pl.ds(1, 31), 0], sem)
-
-    def wait_rest(sem):
-        @pl.when(twice)
-        def _():
-            wait(take.at[0, pl.ds(1, 19)], sem)
-
-        @pl.when(jnp.logical_not(twice))
-        def _():
-            wait(take.at[pl.ds(0, 3), pl.ds(0, 13), 0], sem)
-
-    def block_step(b, carry):
-        @pl.when(b > 0)
-        def _():
-            need_block(p_all, p_recv, b)
-            total = jnp.dot(rounded[b], p_all[b], preferred_element_type=F32)
-            store_part(part.at[b], total)
-
+    def adds_up(ch, which):
+        has = which == -1
+        for k in TURNS[ch]:
+            has = jnp.logical_or(has, which == k)
+        return has
+
+    def tile_of(ch, which):
+        tile = 0
+        for k, t in TURNS[ch].items():
+            tile = jnp.where(which == k, t, tile)
+        return tile
+
+    def wait_rest(ch, sem):
+        count = len(TURNS[ch]) * NZ
+        mine = adds_up(ch, my_class)
+
+        @pl.when(mine)
+        def _():
+            wait(take.at[ch, 0, pl.ds(0, count - 1)], sem)
+
+        @pl.when(jnp.logical_not(mine))
+        def _():
+            wait(take.at[ch, 0, pl.ds(0, count)], sem)
+
+    def send_part(ch, b):
         for dy, dz in moves:
             yy, zz = lax.rem(y + dy, NY), lax.rem(z + dz, NZ)
-            tile = lax.rem(yy - zz + 2 * NZ, NY) + 1
-            to, slot = (g, yy * NZ + zz), dy * NZ + dz
-
-            @pl.when(tile == 1)
-            def _():
-                pair = pl.ds(0, 2)
+            which = lax.rem(my_class + dy - dz + 2 * NZ, NY)
+
+            @pl.when(adds_up(ch, which))
+            def _():
                 remote(
-                    part.at[b, zz, pair], take.at[b, slot, pair], rs_send.at[b],
-                    rs_recv.at[b], to,
+                    part.at[b, zz, tile_of(ch, which)], take.at[ch, b, dy * NZ + dz],
+                    rs_send.at[ch, b], rs_recv.at[ch, b], (g, yy * NZ + zz),
                 ).start()
 
-            @pl.when(tile > 1)
-            def _():
-                remote(
-                    part.at[b, zz, tile], take.at[b, slot, 1], rs_send.at[b],
-                    rs_recv.at[b], to,
-                ).start()
-
-        @pl.when(b == 0)
-        def _():
-            pass_on(*a_way, b)
-
-        @pl.when(b > 0)
-        def _():
-            pass_across(*a_way, b)
-
-            @pl.when(b < BLOCKS - 1)
-            def _():
-                pass_on(*p_way, b + 1)
-
-        wait_each(rs_recv.at[b])
-
-        def add_up(tile, slot):
+    def add_up(ch, b):
+        @pl.when(adds_up(ch, my_class))
+        def _():
+            wait(take.at[ch, b, pl.ds(1, 31)], rs_recv.at[ch, b])
+            tile = tile_of(ch, my_class)
             total = part[b, z, tile].astype(F32)
-            total += jnp.sum(take[b, 1:, slot].astype(F32), axis=0)
+            total += jnp.sum(take[ch, b, 1:].astype(F32), axis=0)
             coef_all[b, z, tile] = total.astype(BF16)
-
-        def spread(ref):
+            ref = coef_all.at[b, z, tile]
             for dy, dz in moves:
                 yy, zz = lax.rem(y + dy, NY), lax.rem(z + dz, NZ)
-                remote(ref, ref, ag_send.at[b], ag_recv.at[b], (g, yy * NZ + zz)).start()
-
-        add_up(my_tile, 1)
-
-        @pl.when(twice)
-        def _():
-            add_up(0, 0)
-            spread(coef_all.at[b, z, pl.ds(0, 2)])
-
-        @pl.when(jnp.logical_not(twice))
-        def _():
-            spread(coef_all.at[b, z, my_tile])
+                remote(
+                    ref, ref, ag_send.at[ch, b], ag_recv.at[ch, b], (g, yy * NZ + zz)
+                ).start()
+
+    def rows_of(ch):
+        first, count = CHAINS[ch]
+        return slice(16 * first, 16 * (first + count))
+
+    def update(ch, b):
+        first, count = CHAINS[ch]
+        rows = rows_of(ch)
+        weights = jnp.concatenate(
+            [
+                coef_all[b, k, first:first + count].reshape(16 * count, LANES)
+                for k in range(NZ)
+            ],
+            axis=1,
+        )
+        change = lax.dot_general(
+            weights, a_all[b], (((1,), (1,)), ((), ())), preferred_element_type=F32
+        )
+        remaining = chain[rows, :] - change
+        chain[rows, :] = remaining
+        rounded[b + 1, rows, :] = remaining.astype(BF16)
+        return remaining.astype(BF16)
+
+    def next_part(ch, b, rows):
+        first, count = CHAINS[ch]
+        total = jnp.dot(rows, p_all[b], preferred_element_type=F32)
+        for k in range(NZ):
+            part[b, k, first:first + count] = (
+                total[:, k * LANES:(k + 1) * LANES].astype(BF16).reshape(count, 16, LANES)
+            )
+
+    for ch in (0, 1):
+        send_part(ch, 0)
+
+    def block_step(b, carry):
+        @pl.when(b == 0)
+        def _():
+            pass_on(*a_way, b)
+
+        @pl.when(b > 0)
+        def _():
+            pass_across(*a_way, b)
+
+            @pl.when(b < BLOCKS - 1)
+            def _():
+                pass_on(*p_way, b + 1)
+
+        for ch in (0, 1):
+            add_up(ch, b)
 
         @pl.when(b == 0)
         def _():
@@ -272,19 +294,23 @@
 
         need_block(a_all, a_recv, b)
 
-        wait_rest(ag_recv.at[b])
-
-        @pl.when(b != g)
-        def _():
-            remote(coef_all.at[b], coef_in.at[g], c_send.at[b], c_recv.at[g], (b, r)).start()
-
-        weights = join(coef_all[b])
-        change = lax.dot_general(
-            weights, a_all[b], (((1,), (1,)), ((), ())), preferred_element_type=F32
-        )
-        remaining = chain[...] - change
-        chain[...] = remaining
-        rounded[b + 1] = remaining.astype(BF16)
+        for ch in (0, 1):
+            wait_rest(ch, ag_recv.at[ch, b])
+            if ch == 1:
+                @pl.when(b != g)
+                def _():
+                    remote(
+                        coef_all.at[b], coef_in.at[g], c_send.at[b], c_recv.at[g], (b, r)
+                    ).start()
+
+            rows = update(ch, b)
+
+            @pl.when(b < BLOCKS - 1)
+            def _():
+                if ch == 0:
+                    need_block(p_all, p_recv, b + 1)
+                next_part(ch, b + 1, rows)
+                send_part(ch, b + 1)
 
         @pl.when(b != g)
         def _():
@@ -340,8 +366,12 @@
         wait(p_all.at[pl.ds(0, 5), pl.ds(0, ROWS // 2)], fwd_send.at[0])
 
     def drain(b, carry):
-        wait_rest(rs_send.at[b])
-        wait_each(ag_send.at[b])
+        for ch in (0, 1):
+            wait_rest(ch, rs_send.at[ch, b])
+
+            @pl.when(adds_up(ch, my_class))
+            def _():
+                wait(take.at[ch, b, pl.ds(1, 31)], ag_send.at[ch, b])
 
         @pl.when(b != g)
         def _():
@@ -376,13 +406,13 @@
             pltpu.VMEM((BLOCKS + 1, WIDE, ROWS), BF16),
             pltpu.VMEM((BLOCKS - 1,) + tiles, BF16),
             pltpu.VMEM((BLOCKS,) + tiles, BF16),
-            pltpu.VMEM((BLOCKS, 32, 2, 16, LANES), BF16),
+            pltpu.VMEM((2, BLOCKS, 32, 16, LANES), BF16),
             pltpu.VMEM((BLOCKS,) + tiles, BF16),
             pltpu.VMEM((BLOCKS,) + tiles, BF16),
             pltpu.VMEM((BLOCKS, WIDE, ROWS), BF16),
             sem((2 + CHUNKS,)), sem, sem, sem((2,)), sem((2,)),
             sem((BLOCKS,)), sem((BLOCKS,)),
-        ] + [sem((BLOCKS,))] * 8,
+        ] + [sem((2, BLOCKS))] * 4 + [sem((BLOCKS,))] * 4,
         compiler_params=pltpu.CompilerParams(
             collective_id=0, has_side_effects=True, vmem_limit_bytes=48 * 2**20
         ),

time: 152 us -> 145 us (0.954)
  Pallas kernels: 147 us -> 140 us
    pallas_call x1, Pallas kernels: 147 us -> 140 us  [local(): pl.pallas_call(sweep_kernel, name='block_sweep', out_shape=(jax.ShapeDtyp...]
where the time goes in v4:
time: 145 us
  Pallas kernels  140 us (97%)
  local copies, waits for them, and re-layouts  4.32 us (3%)
    pallas_call x1, Pallas kernels, local(): pl.pallas_call(sweep_kernel, name='block_sweep', out_shape=(jax.ShapeDtyp...  140 us
    unnamed x6, local copies, waits for them, and re-layouts  4.32 us

profile of v4, /device:TPU:7, one launch (start us, length us, event | category | flops | bytes accessed | tf_op | source)
XLA Modules:
  0.0 144.9 jit_solution(7138051112935043579)
XLA Ops:
  0.6 0.0 copy-start
  0.6 1.1 copy-done
  1.7 0.0 copy-start.1
  1.7 1.0 copy-done.1
  2.7 139.9 %block_sweep.1 = (f32[576,1024]{1,0:T(8,128)S(1)}, f32[576,256]{1,0:T(8,128)S(1)}) custom-call(bf16[256,1024]{1,0:T(8,128)(2,1)S(1)} %copy-done.1, f32[576,256]{1,0:T(8,128)S(1)} %bitcast.7, f32[1024,1024]{1,0:T(8,128)} %prec_hbm.1), custom_call_target="tpu_custom_call" | custom-call | flops 2000000000 | bytes 8000000 | tf_op jit(solution)/shard_map/block_sweep/pallas_call | solution.py:391
  142.6 1.4 copy.7
  144.0 0.8 copy.8
Async XLA Ops:
  0.6 1.1 copy-start
  1.7 1.0 copy-start.1

commit v5 on v4

--- a/solution.py
+++ b/solution.py
@@ -146,7 +146,7 @@
         if j == 0:
             pl.semaphore_wait(barrier, len(others))
 
-            @pl.when(g > 1)
+            @pl.when(g > 0)
             def _():
                 send_own(a_all, a_recv, own_send.at[1])
 
@@ -178,7 +178,7 @@
     def _():
         send_own(p_all, p_recv, own_send.at[0])
 
-    @pl.when(g < 2)
+    @pl.when(g == 0)
     def _():
         send_own(a_all, a_recv, own_send.at[1])
 

time: 145 us -> 144 us (level)
  no operation moved by 1% of the time
where the time goes in v5:
time: 144 us
  Pallas kernels  139 us (97%)
  local copies, waits for them, and re-layouts  4.32 us (3%)
    pallas_call x1, Pallas kernels, local(): pl.pallas_call(sweep_kernel, name='block_sweep', out_shape=(jax.ShapeDtyp...  139 us
    unnamed x6, local copies, waits for them, and re-layouts  4.32 us

profile of v5, /device:TPU:7, one launch (start us, length us, event | category | flops | bytes accessed | tf_op | source)
XLA Modules:
  0.0 143.8 jit_solution(9136681324649466679)
XLA Ops:
  0.6 0.0 copy-start
  0.6 1.1 copy-done
  1.7 0.0 copy-start.1
  1.7 1.0 copy-done.1
  2.7 138.8 %block_sweep.1 = (f32[576,1024]{1,0:T(8,128)S(1)}, f32[576,256]{1,0:T(8,128)S(1)}) custom-call(bf16[256,1024]{1,0:T(8,128)(2,1)S(1)} %copy-done.1, f32[576,256]{1,0:T(8,128)S(1)} %bitcast.7, f32[1024,1024]{1,0:T(8,128)} %prec_hbm.1), custom_call_target="tpu_custom_call" | custom-call | flops 2000000000 | bytes 8000000 | tf_op jit(solution)/shard_map/block_sweep/pallas_call | solution.py:391
  141.6 1.4 copy.7
  143.0 0.8 copy.8
Async XLA Ops:
  0.6 1.1 copy-start
  1.7 1.0 copy-start.1

commit v6 on v5

--- a/solution.py
+++ b/solution.py
@@ -39,7 +39,7 @@
 def sweep_kernel(
     feat_hbm, resid_hbm, prec_hbm, coef_out, sect_out,
     a_all, p_all, prec, resid, chain, rounded, first, part, take,
-    coef_all, coef_in, chain_in,
+    coef_all, coef_in, chain_in, turned,
     load_sem, first_send, first_recv, own_send, fwd_send, p_recv, a_recv,
     rs_send, rs_recv, ag_send, ag_recv, c_send, c_recv, r_send, r_recv,
 ):
@@ -247,9 +247,7 @@
             ],
             axis=1,
         )
-        change = lax.dot_general(
-            weights, a_all[b], (((1,), (1,)), ((), ())), preferred_element_type=F32
-        )
+        change = jnp.dot(weights, turned[...], preferred_element_type=F32)
         remaining = chain[rows, :] - change
         chain[rows, :] = remaining
         rounded[b + 1, rows, :] = remaining.astype(BF16)
@@ -293,6 +291,7 @@
             pass_on(*a_way, b + 1)
 
         need_block(a_all, a_recv, b)
+        turned[...] = a_all[b].T
 
         for ch in (0, 1):
             wait_rest(ch, ag_recv.at[ch, b])
@@ -410,6 +409,7 @@
             pltpu.VMEM((BLOCKS,) + tiles, BF16),
             pltpu.VMEM((BLOCKS,) + tiles, BF16),
             pltpu.VMEM((BLOCKS, WIDE, ROWS), BF16),
+            pltpu.VMEM((BLK, ROWS), BF16),
             sem((2 + CHUNKS,)), sem, sem, sem((2,)), sem((2,)),
             sem((BLOCKS,)), sem((BLOCKS,)),
         ] + [sem((2, BLOCKS))] * 4 + [sem((BLOCKS,))] * 4,

time: 144 us -> 144 us (level)
  no operation moved by 1% of the time
where the time goes in v6:
time: 144 us
  Pallas kernels  139 us (97%)
  local copies, waits for them, and re-layouts  4.32 us (3%)
    pallas_call x1, Pallas kernels, local(): pl.pallas_call(sweep_kernel, name='block_sweep', out_shape=(jax.ShapeDtyp...  139 us
    unnamed x6, local copies, waits for them, and re-layouts  4.32 us

profile of v6, /device:TPU:7, one launch (start us, length us, event | category | flops | bytes accessed | tf_op | source)
XLA Modules:
  0.0 144.0 jit_solution(3593044530983388026)
XLA Ops:
  0.6 0.0 copy-start
  0.6 1.1 copy-done
  1.7 0.0 copy-start.1
  1.7 1.0 copy-done.1
  2.7 139.0 %block_sweep.1 = (f32[576,1024]{1,0:T(8,128)S(1)}, f32[576,256]{1,0:T(8,128)S(1)}) custom-call(bf16[256,1024]{1,0:T(8,128)(2,1)S(1)} %copy-done.1, f32[576,256]{1,0:T(8,128)S(1)} %bitcast.7, f32[1024,1024]{1,0:T(8,128)} %prec_hbm.1), custom_call_target="tpu_custom_call" | custom-call | flops 2000000000 | bytes 8000000 | tf_op jit(solution)/shard_map/block_sweep/pallas_call | solution.py:390
  141.8 1.4 copy.7
  143.2 0.8 copy.8
Async XLA Ops:
  0.6 1.1 copy-start
  1.7 1.0 copy-start.1
